TPU v7x, 256 devices: a whole 4x4x8 slice. The times are simulated.
256 devices in a mesh: gx: 8 (over y, core), gy: 8 (over z_hi, x), af: 4 (over z_lo).
Axes of the slice: x: 4, y: 4, z: 8 (z_hi: 2, z_lo: 4; z = z_hi * 4 + z_lo), core: 2. Of those that a mesh axis runs over, the one named last changes fastest.
Arguments:
- volume: bfloat16 [32, 32, 128, 128], P('af', 'gx', 'gy'), may hold values from -6 to 6
- weight_one: bfloat16 [32, 32, 3, 3, 3], P('af'), may hold values from -0.21875 to 0.21875
- bias_one: float32 [32], P('af'), may hold values from -1 to 1
- weight_two: bfloat16 [32, 32, 3, 3, 3], P('af'), may hold values from -0.21875 to 0.21875
- cotangent: bfloat16 [32, 32, 128, 128], P('af', 'gx', 'gy'), may hold values from -6 to 6
Outputs:
- output: bfloat16 [32, 32, 128, 128], P('af', 'gx', 'gy')
- input_grad: bfloat16 [32, 32, 128, 128], P('af', 'gx', 'gy')
- grad_one: float32 [32, 32, 3, 3, 3], P('af')
- bias_grad: float32 [32], P('af')
- grad_two: float32 [32, 32, 3, 3, 3], P('af')
All inputs are finite; a program needn't handle non-finite values.
Results may differ from a plain program's by a relative error of at most 0.0065.
Values may be sent and summed in bfloat16 or wider, within the bound.
A program may use at most 64 MiB of HBM per device.

v0:
```python
import math
import jax
import jax.numpy as jnp
from jax import lax
from jax.sharding import PartitionSpec as P


def with_halo(cells, sides, width):
    for axis, dim in sides:
        count = lax.axis_size(axis)
        ends = count - 1
        head = lax.slice_in_dim(cells, 0, width, axis=dim)
        tail = lax.slice_in_dim(cells, cells.shape[dim] - width, cells.shape[dim], axis=dim)
        cells = jnp.concatenate(
            [
                lax.ppermute(tail, axis, [(i, (i + 1) % count) for i in range(ends)]),
                cells,
                lax.ppermute(head, axis, [((i + 1) % count, i) for i in range(ends)]),
            ],
            axis=dim,
        )
    return cells


def conv_valid(padded, weight):
    size_x = padded.shape[1] - 2
    size_y = padded.shape[2] - 2
    size_z = padded.shape[3] - 2
    total = jnp.zeros((weight.shape[0], size_x, size_y, size_z), jnp.float32)
    for off_x in range(3):
        for off_y in range(3):
            for off_z in range(3):
                window = padded[
                    :, off_x : off_x + size_x, off_y : off_y + size_y, off_z : off_z + size_z
                ]
                total = total + jnp.einsum(
                    "oi,ixyz->oxyz",
                    weight[:, :, off_x, off_y, off_z],
                    window,
                    preferred_element_type=jnp.float32,
                )
    return total


def kernel_grad(padded, cot_field):
    size_x = cot_field.shape[1]
    size_y = cot_field.shape[2]
    size_z = cot_field.shape[3]
    blocks = []
    for off_x in range(3):
        for off_y in range(3):
            for off_z in range(3):
                window = padded[
                    :, off_x : off_x + size_x, off_y : off_y + size_y, off_z : off_z + size_z
                ]
                blocks.append(
                    jnp.einsum(
                        "oxyz,ixyz->oi", cot_field, window, preferred_element_type=jnp.float32
                    )
                )
    stacked = jnp.stack(blocks, axis=-1)
    return stacked.reshape(cot_field.shape[0], padded.shape[0], 3, 3, 3)


def flipped(weight):
    return jnp.transpose(jnp.flip(weight, (2, 3, 4)), (1, 0, 2, 3, 4))


def depth_pad(values):
    return jnp.pad(values, ((0, 0), (0, 0), (0, 0), (1, 1)))


def full_padded(values):
    gathered = lax.all_gather(values, "af", axis=0, tiled=True)
    rimmed = with_halo(gathered, (("gx", 1), ("gy", 2)), 1)
    return depth_pad(rimmed)


def silu_grad(hidden_grad, pre_act):
    sigma_vals = jax.nn.sigmoid(pre_act)
    return (hidden_grad * sigma_vals * (1.0 + pre_act * (1.0 - sigma_vals))).astype(jnp.bfloat16)


def body(volume, weight_one, bias_one, weight_two, cotangent):
    own_rows = volume.shape[0]
    vol_pad = full_padded(volume)
    pre_act = conv_valid(vol_pad, weight_one) + bias_one[:, None, None, None]
    hidden = jax.nn.silu(pre_act).astype(jnp.bfloat16)
    hid_pad = full_padded(hidden)
    output = conv_valid(hid_pad, weight_two).astype(jnp.bfloat16)
    local_two = kernel_grad(hid_pad, cotangent)
    every_one, every_two = (
        lax.all_gather(weight_one, "af", axis=0, tiled=True),
        lax.all_gather(weight_two, "af", axis=0, tiled=True),
    )
    first_row = lax.axis_index("af") * own_rows

    def transposed(cot_field, every_w):
        padded = full_padded(cot_field)
        turned = lax.dynamic_slice_in_dim(flipped(every_w), first_row, own_rows, 0)
        return conv_valid(padded, turned)

    hidden_grad = transposed(cotangent, every_two)
    pre_grad = silu_grad(hidden_grad, pre_act)
    local_one = kernel_grad(vol_pad, pre_grad)
    local_bias = jnp.sum(pre_grad, axis=(1, 2, 3), dtype=jnp.float32)
    input_grad = transposed(pre_grad, every_one).astype(jnp.bfloat16)
    summed_one, summed_bias, summed_two = lax.psum((local_one, local_bias, local_two), ("gx", "gy"))
    cell_total = (
        volume.shape[1]
        * lax.axis_size("gx")
        * volume.shape[2]
        * lax.axis_size("gy")
        * volume.shape[3]
    )
    grad_scale = 1.0 / math.sqrt(cell_total)
    return (
        output,
        input_grad,
        summed_one * grad_scale,
        summed_bias * grad_scale,
        summed_two * grad_scale,
    )


def solution(mesh):
    return jax.shard_map(
        body,
        mesh=mesh,
        in_specs=(
            P("af", "gx", "gy", None),
            P("af", None, None, None, None),
            P("af"),
            P("af", None, None, None, None),
            P("af", "gx", "gy", None),
        ),
        out_specs=(
            P("af", "gx", "gy", None),
            P("af", "gx", "gy", None),
            P("af", None, None, None, None),
            P("af"),
            P("af", None, None, None, None),
        ),
        check_vma=False,
    )
```

profile of v0, /device:TPU:0, one launch (start us, length us, event | category | flops | bytes accessed | tf_op | source)
XLA Modules:
  0.0 645.6 jit_solution(11498958030644135914)
XLA Ops:
  1.7 14.6 %all_gather.18 = bf16[32,4,16,128]{3,0,2,1:T(8,128)(2,1)S(1)} all-gather(bf16[8,4,16,128]{3,0,2,1:T(8,128)(2,1)S(1)} %copy.43), channel_id=1, replica_groups=mesh['gx'=8,'gy'=8,'af'=4] {'af'}, dimensions={0}, use_global_device_ids=true | all-gather | bytes 655360 | tf_op jit(solution)/shard_map/all_gather | solution.py:74
  16.3 1.3 collective-permute-start
  17.6 1.3 collective-permute-start.1
  19.9 15.3 %all_gather.22 = bf16[32,4,16,128]{3,0,2,1:T(8,128)(2,1)S(1)} all-gather(bf16[8,4,16,128]{3,0,2,1:T(8,128)(2,1)S(1)} %copy.46), channel_id=1, replica_groups=mesh['gx'=8,'gy'=8,'af'=4] {'af'}, dimensions={0}, use_global_device_ids=true | all-gather | bytes 655360 | tf_op jit(solution)/shard_map/all_gather | solution.py:74
  35.2 2.1 collective-permute-start.8
  37.4 1.3 collective-permute-start.9
  38.9 13.0 %all_gather.21 = bf16[32,32,3,3,3]{1,0,4,3,2:T(8,128)(2,1)S(1)} all-gather(bf16[8,32,3,3,3]{1,0,4,3,2:T(8,128)(2,1)S(1)} %copy-done.48), channel_id=1, replica_groups=mesh['gx'=8,'gy'=8,'af'=4] {'af'}, dimensions={0}, use_global_device_ids=true | all-gather | bytes 69120 | tf_op jit(solution)/shard_map/all_gather | solution.py:94
  52.3 13.0 %all_gather.20 = bf16[32,32,3,3,3]{1,0,4,3,2:T(8,128)(2,1)S(1)} all-gather(bf16[8,32,3,3,3]{1,0,4,3,2:T(8,128)(2,1)S(1)} %copy-done.50), channel_id=1, replica_groups=mesh['gx'=8,'gy'=8,'af'=4] {'af'}, dimensions={0}, use_global_device_ids=true | all-gather | bytes 69120 | tf_op jit(solution)/shard_map/all_gather | solution.py:93
  66.0 3.4 collective-permute-start.2
  69.4 1.3 collective-permute-start.3
  71.2 4.5 collective-permute-start.10
  75.8 1.5 collective-permute-start.11
  92.0 15.4 %all_gather.23 = bf16[32,4,16,128]{3,0,2,1:T(8,128)(2,1)S(1)} all-gather(bf16[8,4,16,128]{3,0,2,1:T(8,128)(2,1)S(1)} %get-tuple-element.51), channel_id=1, replica_groups=mesh['gx'=8,'gy'=8,'af'=4] {'af'}, dimensions={0}, use_global_device_ids=true | all-gather | bytes 655360 | tf_op jit(solution)/shard_map/all_gather | solution.py:74
  107.4 14.4 %all_gather.19 = bf16[32,4,16,128]{3,0,2,1:T(8,128)(2,1)S(1)} all-gather(bf16[8,4,16,128]{3,0,2,1:T(8,128)(2,1)S(1)} %get-tuple-element.48), channel_id=1, replica_groups=mesh['gx'=8,'gy'=8,'af'=4] {'af'}, dimensions={0}, use_global_device_ids=true | all-gather | bytes 655360 | tf_op jit(solution)/shard_map/all_gather | solution.py:74
  123.9 1.5 collective-permute-start.5
  132.2 8.9 %collective-permute-start.12 = (bf16[32,1,16,128]{3,0,2,1:T(8,128)(2,1)S(1)}, bf16[32,1,16,128]{3,0,2,1:T(8,128)(2,1)S(1)}, u32[]{:S(2)}, u32[]{:S(2)}) collective-permute-start(bf16[32,1,16,128]{3,0,2,1:T(8,128)(2,1)S(1)} %get-tuple-element.27), channel_id=1, source_target_pairs={{0,32},{32,64},{64,96},{96,128},{128,160},{160,192},{192,224},{1,3... | collective-permute-start | bytes 393224 | tf_op jit(solution)/shard_map/ppermute | solution.py:16
  141.1 1.3 collective-permute-start.13
  144.3 4.4 collective-permute-start.6
  148.7 1.3 collective-permute-start.7
  150.2 9.7 %collective-permute-start.14 = (bf16[32,6,1,128]{3,0,2,1:T(8,128)(2,1)S(1)}, bf16[32,6,1,128]{3,0,2,1:T(8,128)(2,1)S(1)}, u32[]{:S(2)}, u32[]{:S(2)}) collective-permute-start(bf16[32,6,1,128]{3,0,2,1:T(8,128)(2,1)S(1)} %get-tuple-element.18), channel_id=1, source_target_pairs={{0,4},{4,8},{8,12},{12,16},{16,20},{20,24},{24,28},{1,5},{5,9},{9,... | collective-permute-start | bytes 147464 | tf_op jit(solution)/shard_map/ppermute | solution.py:16
  160.0 1.3 collective-permute-start.15
  164.8 7.0 %collective-permute-done.15 = bf16[32,6,1,128]{3,0,2,1:T(8,128)(2,1)S(1)} collective-permute-done((bf16[32,6,1,128]{3,0,2,1:T(8,128)(2,1)S(1)}, bf16[32,6,1,128]{3,0,2,1:T(8,128)(2,1)S(1)}, u32[]{:S(2)}, u32[]{:S(2)}) %collective-permute-start.15) | collective-permute-done | bytes 49184 | tf_op jit(solution)/shard_map/ppermute | solution.py:18
  213.4 413.0 %all-reduce.4 = (f32[8,32,3,3,3]{1,0,4,3,2:T(8,128)}, f32[8]{0:T(128)S(1)}, f32[8,32,3,3,3]{1,0,4,3,2:T(8,128)}) all-reduce(f32[8,32,3,3,3]{1,0,4,3,2:T(8,128)} %bitcast.1393, f32[8]{0:T(128)S(1)} %get-tuple-element.50, f32[8,32,3,3,3]{1,0,4,3,2:T(8,128)} %bitcast.1394), channel_id=1, replica_groups=mesh['gx'=8,'gy'=8,'af'=4] {'gx','gy'}, use_global_device_ids=true, to_apply=%region_0.1 | all-reduce | flops 13832 | bytes 110656 | tf_op jit(solution)/shard_map/psum | solution.py:108
  627.0 1.4 fusion.187
  (333 shorter events, 91.5 us)
Async XLA Ops:
  0.6 38.1 %copy-start.50 = (bf16[8,32,3,3,3]{1,0,4,3,2:T(8,128)(2,1)S(1)}, bf16[8,32,3,3,3]{1,0,4,3,2:T(8,128)(2,1)}, u32[]{:S(2)}) copy-start(bf16[8,32,3,3,3]{1,0,4,3,2:T(8,128)(2,1)} %param.6) | copy-start | bytes 41476
  1.7 37.2 %copy-start.48 = (bf16[8,32,3,3,3]{1,0,4,3,2:T(8,128)(2,1)S(1)}, bf16[8,32,3,3,3]{1,0,4,3,2:T(8,128)(2,1)}, u32[]{:S(2)}) copy-start(bf16[8,32,3,3,3]{1,0,4,3,2:T(8,128)(2,1)} %param.8) | copy-start | bytes 41476
  16.3 49.2 %collective-permute-start = (bf16[32,1,16,128]{3,0,2,1:T(8,128)(2,1)S(1)}, bf16[32,1,16,128]{3,0,2,1:T(8,128)(2,1)S(1)}, u32[]{:S(2)}, u32[]{:S(2)}) collective-permute-start(bf16[32,1,16,128]{3,0,2,1:T(8,128)(2,1)S(1)} %get-tuple-element.39), channel_id=1, source_target_pairs={{0,32},{32,64},{64,96},{96,128},{128,160},{160,192},{192,224},{1,3... | collective-permute-start | bytes 393224 | tf_op jit(solution)/shard_map/ppermute | solution.py:16
  17.6 48.3 %collective-permute-start.1 = (bf16[32,1,16,128]{3,0,2,1:T(8,128)(2,1)S(1)}, bf16[32,1,16,128]{3,0,2,1:T(8,128)(2,1)S(1)}, u32[]{:S(2)}, u32[]{:S(2)}) collective-permute-start(bf16[32,1,16,128]{3,0,2,1:T(8,128)(2,1)S(1)} %get-tuple-element.38), channel_id=1, source_target_pairs={{32,0},{64,32},{96,64},{128,96},{160,128},{192,160},{224,192},{33,... | collective-permute-start | bytes 393224 | tf_op jit(solution)/shard_map/ppermute | solution.py:18
  35.2 35.8 %collective-permute-start.8 = (bf16[32,1,16,128]{3,0,2,1:T(8,128)(2,1)S(1)}, bf16[32,1,16,128]{3,0,2,1:T(8,128)(2,1)S(1)}, u32[]{:S(2)}, u32[]{:S(2)}) collective-permute-start(bf16[32,1,16,128]{3,0,2,1:T(8,128)(2,1)S(1)} %get-tuple-element.29), channel_id=1, source_target_pairs={{0,32},{32,64},{64,96},{96,128},{128,160},{160,192},{192,224},{1,3... | collective-permute-start | bytes 393224 | tf_op jit(solution)/shard_map/ppermute | solution.py:16
  37.4 33.8 %collective-permute-start.9 = (bf16[32,1,16,128]{3,0,2,1:T(8,128)(2,1)S(1)}, bf16[32,1,16,128]{3,0,2,1:T(8,128)(2,1)S(1)}, u32[]{:S(2)}, u32[]{:S(2)}) collective-permute-start(bf16[32,1,16,128]{3,0,2,1:T(8,128)(2,1)S(1)} %get-tuple-element.28), channel_id=1, source_target_pairs={{32,0},{64,32},{96,64},{128,96},{160,128},{192,160},{224,192},{33,... | collective-permute-start | bytes 393224 | tf_op jit(solution)/shard_map/ppermute | solution.py:18
  65.5 121.7 %copy-start.47 = (bf16[8,32,3,3,3]{1,0,4,3,2:T(8,128)(2,1)}, bf16[8,32,3,3,3]{1,0,4,3,2:T(8,128)(2,1)S(1)}, u32[]{:S(2)}) copy-start(bf16[8,32,3,3,3]{1,0,4,3,2:T(8,128)(2,1)S(1)} %dynamic-slice_bitcast_fusion.1) | copy-start | bytes 41476
  66.0 11.6 %collective-permute-start.2 = (bf16[32,6,1,128]{3,0,2,1:T(8,128)(2,1)S(1)}, bf16[32,6,1,128]{3,0,2,1:T(8,128)(2,1)S(1)}, u32[]{:S(2)}, u32[]{:S(2)}) collective-permute-start(bf16[32,6,1,128]{3,0,2,1:T(8,128)(2,1)S(1)} %get-tuple-element.24), channel_id=1, source_target_pairs={{0,4},{4,8},{8,12},{12,16},{16,20},{20,24},{24,28},{1,5},{5,9},{9,... | collective-permute-start | bytes 147464 | tf_op jit(solution)/shard_map/ppermute | solution.py:16
  69.4 8.3 %collective-permute-start.3 = (bf16[32,6,1,128]{3,0,2,1:T(8,128)(2,1)S(1)}, bf16[32,6,1,128]{3,0,2,1:T(8,128)(2,1)S(1)}, u32[]{:S(2)}, u32[]{:S(2)}) collective-permute-start(bf16[32,6,1,128]{3,0,2,1:T(8,128)(2,1)S(1)} %get-tuple-element.25), channel_id=1, source_target_pairs={{4,0},{8,4},{12,8},{16,12},{20,16},{24,20},{28,24},{5,1},{9,5},{13... | collective-permute-start | bytes 147464 | tf_op jit(solution)/shard_map/ppermute | solution.py:18
  71.2 11.8 %collective-permute-start.10 = (bf16[32,6,1,128]{3,0,2,1:T(8,128)(2,1)S(1)}, bf16[32,6,1,128]{3,0,2,1:T(8,128)(2,1)S(1)}, u32[]{:S(2)}, u32[]{:S(2)}) collective-permute-start(bf16[32,6,1,128]{3,0,2,1:T(8,128)(2,1)S(1)} %get-tuple-element.20), channel_id=1, source_target_pairs={{0,4},{4,8},{8,12},{12,16},{16,20},{20,24},{24,28},{1,5},{5,9},{9,... | collective-permute-start | bytes 147464 | tf_op jit(solution)/shard_map/ppermute | solution.py:16
  75.8 7.3 %collective-permute-start.11 = (bf16[32,6,1,128]{3,0,2,1:T(8,128)(2,1)S(1)}, bf16[32,6,1,128]{3,0,2,1:T(8,128)(2,1)S(1)}, u32[]{:S(2)}, u32[]{:S(2)}) collective-permute-start(bf16[32,6,1,128]{3,0,2,1:T(8,128)(2,1)S(1)} %get-tuple-element.21), channel_id=1, source_target_pairs={{4,0},{8,4},{12,8},{16,12},{20,16},{24,20},{28,24},{5,1},{9,5},{13... | collective-permute-start | bytes 147464 | tf_op jit(solution)/shard_map/ppermute | solution.py:18
  122.7 21.2 %collective-permute-start.4 = (bf16[32,1,16,128]{3,0,2,1:T(8,128)(2,1)S(1)}, bf16[32,1,16,128]{3,0,2,1:T(8,128)(2,1)S(1)}, u32[]{:S(2)}, u32[]{:S(2)}) collective-permute-start(bf16[32,1,16,128]{3,0,2,1:T(8,128)(2,1)S(1)} %get-tuple-element.34), channel_id=1, source_target_pairs={{0,32},{32,64},{64,96},{96,128},{128,160},{160,192},{192,224},{1,3... | collective-permute-start | bytes 393224 | tf_op jit(solution)/shard_map/ppermute | solution.py:16
  123.9 20.3 %collective-permute-start.5 = (bf16[32,1,16,128]{3,0,2,1:T(8,128)(2,1)S(1)}, bf16[32,1,16,128]{3,0,2,1:T(8,128)(2,1)S(1)}, u32[]{:S(2)}, u32[]{:S(2)}) collective-permute-start(bf16[32,1,16,128]{3,0,2,1:T(8,128)(2,1)S(1)} %get-tuple-element.33), channel_id=1, source_target_pairs={{32,0},{64,32},{96,64},{128,96},{160,128},{192,160},{224,192},{33,... | collective-permute-start | bytes 393224 | tf_op jit(solution)/shard_map/ppermute | solution.py:18
  132.2 17.8 %collective-permute-start.12 = (bf16[32,1,16,128]{3,0,2,1:T(8,128)(2,1)S(1)}, bf16[32,1,16,128]{3,0,2,1:T(8,128)(2,1)S(1)}, u32[]{:S(2)}, u32[]{:S(2)}) collective-permute-start(bf16[32,1,16,128]{3,0,2,1:T(8,128)(2,1)S(1)} %get-tuple-element.27), channel_id=1, source_target_pairs={{0,32},{32,64},{64,96},{96,128},{128,160},{160,192},{192,224},{1,3... | collective-permute-start | bytes 393224 | tf_op jit(solution)/shard_map/ppermute | solution.py:16
  141.1 9.1 %collective-permute-start.13 = (bf16[32,1,16,128]{3,0,2,1:T(8,128)(2,1)S(1)}, bf16[32,1,16,128]{3,0,2,1:T(8,128)(2,1)S(1)}, u32[]{:S(2)}, u32[]{:S(2)}) collective-permute-start(bf16[32,1,16,128]{3,0,2,1:T(8,128)(2,1)S(1)} %get-tuple-element.26), channel_id=1, source_target_pairs={{32,0},{64,32},{96,64},{128,96},{160,128},{192,160},{224,192},{33,... | collective-permute-start | bytes 393224 | tf_op jit(solution)/shard_map/ppermute | solution.py:18
  144.3 67.9 %copy-start.3 = (bf16[32,6,16,128]{3,0,2,1:T(8,128)(2,1)}, bf16[32,6,16,128]{3,0,2,1:T(8,128)(2,1)S(1)}, u32[]{:S(2)}) copy-start(bf16[32,6,16,128]{3,0,2,1:T(8,128)(2,1)S(1)} %get-tuple-element.43) | copy-start | bytes 2359300
  144.3 43.9 %collective-permute-start.6 = (bf16[32,6,1,128]{3,0,2,1:T(8,128)(2,1)S(1)}, bf16[32,6,1,128]{3,0,2,1:T(8,128)(2,1)S(1)}, u32[]{:S(2)}, u32[]{:S(2)}) collective-permute-start(bf16[32,6,1,128]{3,0,2,1:T(8,128)(2,1)S(1)} %get-tuple-element.22), channel_id=1, source_target_pairs={{0,4},{4,8},{8,12},{12,16},{16,20},{20,24},{24,28},{1,5},{5,9},{9,... | collective-permute-start | bytes 147464 | tf_op jit(solution)/shard_map/ppermute | solution.py:16
  148.7 39.5 %collective-permute-start.7 = (bf16[32,6,1,128]{3,0,2,1:T(8,128)(2,1)S(1)}, bf16[32,6,1,128]{3,0,2,1:T(8,128)(2,1)S(1)}, u32[]{:S(2)}, u32[]{:S(2)}) collective-permute-start(bf16[32,6,1,128]{3,0,2,1:T(8,128)(2,1)S(1)} %get-tuple-element.23), channel_id=1, source_target_pairs={{4,0},{8,4},{12,8},{16,12},{20,16},{24,20},{28,24},{5,1},{9,5},{13... | collective-permute-start | bytes 147464 | tf_op jit(solution)/shard_map/ppermute | solution.py:18
  150.2 21.7 %copy-start = (bf16[32,6,16,128]{3,0,2,1:T(8,128)(2,1)}, bf16[32,6,16,128]{3,0,2,1:T(8,128)(2,1)S(1)}, u32[]{:S(2)}) copy-start(bf16[32,6,16,128]{3,0,2,1:T(8,128)(2,1)S(1)} %constant_dynamic-update-slice_fusion.17) | copy-start | bytes 2359300
  150.2 14.6 %collective-permute-start.14 = (bf16[32,6,1,128]{3,0,2,1:T(8,128)(2,1)S(1)}, bf16[32,6,1,128]{3,0,2,1:T(8,128)(2,1)S(1)}, u32[]{:S(2)}, u32[]{:S(2)}) collective-permute-start(bf16[32,6,1,128]{3,0,2,1:T(8,128)(2,1)S(1)} %get-tuple-element.18), channel_id=1, source_target_pairs={{0,4},{4,8},{8,12},{12,16},{16,20},{20,24},{24,28},{1,5},{5,9},{9,... | collective-permute-start | bytes 147464 | tf_op jit(solution)/shard_map/ppermute | solution.py:16
  160.0 11.9 %collective-permute-start.15 = (bf16[32,6,1,128]{3,0,2,1:T(8,128)(2,1)S(1)}, bf16[32,6,1,128]{3,0,2,1:T(8,128)(2,1)S(1)}, u32[]{:S(2)}, u32[]{:S(2)}) collective-permute-start(bf16[32,6,1,128]{3,0,2,1:T(8,128)(2,1)S(1)} %get-tuple-element.19), channel_id=1, source_target_pairs={{4,0},{8,4},{12,8},{16,12},{20,16},{24,20},{28,24},{5,1},{9,5},{13... | collective-permute-start | bytes 147464 | tf_op jit(solution)/shard_map/ppermute | solution.py:18
  164.8 9.9 %copy-start.43 = (bf16[32,6,1,128]{3,0,2,1:T(8,128)(2,1)}, bf16[32,6,1,128]{3,0,2,1:T(8,128)(2,1)S(1)}, u32[]{:S(2)}) copy-start(bf16[32,6,1,128]{3,0,2,1:T(8,128)(2,1)S(1)} %collective-permute-done.14) | copy-start | bytes 147460
  188.3 21.9 %copy-start.55 = (bf16[32,6,1,128]{3,0,2,1:T(8,128)(2,1)}, bf16[32,6,1,128]{3,0,2,1:T(8,128)(2,1)S(1)}, u32[]{:S(2)}) copy-start(bf16[32,6,1,128]{3,0,2,1:T(8,128)(2,1)S(1)} %collective-permute-done.6) | copy-start | bytes 147460
  188.3 23.9 %copy-start.57 = (bf16[32,6,1,128]{3,0,2,1:T(8,128)(2,1)}, bf16[32,6,1,128]{3,0,2,1:T(8,128)(2,1)S(1)}, u32[]{:S(2)}) copy-start(bf16[32,6,1,128]{3,0,2,1:T(8,128)(2,1)S(1)} %collective-permute-done.7) | copy-start | bytes 147460
  (52 other events, 146.3 us)
where the time goes:
time: 647 us; the launch traced here: 646 us
  blocking collectives  499 us (77%)
  matrix products  80.8 us (12%)
  starting transfers between devices  46.4 us (7%)
  waiting for transfers between devices  7.08 us (1%)
    psum x1, blocking collectives, body(): lax.psum((local_one, local_bias, local_two), ('gx', 'gy'))  413 us
    dot_general x108, matrix products, conv_valid(): jnp.einsum('oi,ixyz->oxyz', weight[:, :, off_x, off_y, off_z], window, pr...  65.3 us
    all_gather x4, blocking collectives, full_padded(): gathered = lax.all_gather(values, 'af', axis=0, tiled=True)  59.7 us
    ppermute x8, starting transfers between devices, with_halo(): lax.ppermute(tail, axis, [(i, (i + 1) % count) for i in range(ends)])  35.7 us
    dot_general x54, matrix products, kernel_grad(): jnp.einsum('oxyz,ixyz->oi', cot_field, window, preferred_element_type=jnp...  15.6 us
    all_gather x1, blocking collectives, body(): lax.all_gather(weight_one, 'af', axis=0, tiled=True)  13 us
    all_gather x1, blocking collectives, body(): lax.all_gather(weight_two, 'af', axis=0, tiled=True)  13 us
  transfers between devices with their start and end apart: 16, of which 1 were waited for; matrix products, arithmetic and copies ran while one was open for 6% of the time, Pallas kernels for 0%

commit v1 on v0

--- a/solution.py
+++ b/solution.py
@@ -71,7 +71,9 @@
 
 
 def full_padded(values):
-    gathered = lax.all_gather(values, "af", axis=0, tiled=True)
+    gathered = jnp.concatenate(
+        lax.all_to_all(jnp.stack([values] * lax.axis_size("af")), "af", 0, 0), axis=0
+    )
     rimmed = with_halo(gathered, (("gx", 1), ("gy", 2)), 1)
     return depth_pad(rimmed)
 

time: 647 us -> 662 us (1.023)
  blocking collectives: 499 us -> 442 us
  starting transfers between devices: 46.4 us -> 70.3 us
  waiting for transfers between devices: 7.08 us -> 26.1 us
  matrix products: 80.8 us -> 99.3 us
    all_gather x4 -> x0, blocking collectives: 59.7 us -> none  [full_padded(): gathered = lax.all_gather(values, 'af', axis=0, tiled=True)]
    all_to_all x0 -> x4, starting transfers between devices: none -> 26.1 us  [full_padded(): lax.all_to_all(jnp.stack([values] * lax.axis_size('af')), 'af', 0, 0)]
    all_to_all x0 -> x4, waiting for transfers between devices: none -> 22.3 us  [full_padded(): lax.all_to_all(jnp.stack([values] * lax.axis_size('af')), 'af', 0, 0)]
    dot_general x54, matrix products: 15.6 us -> 32.3 us  [kernel_grad(): jnp.einsum('oxyz,ixyz->oi', cot_field, window, preferred_element_type=jnp...]
    all_gather x1, blocking collectives: 13 us -> 20.5 us  [body(): lax.all_gather(weight_one, 'af', axis=0, tiled=True)]
  transfers between devices with their start and end apart: 16 -> 20, of which waited for: 1 -> 4; matrix products, arithmetic and copies ran while one was open for 6% -> 8% of each run, Pallas kernels for 0% -> 0%
where the time goes in v1:
time: 662 us; the launch traced here: 659 us
  blocking collectives  442 us (67%)
  matrix products  99.3 us (15%)
  starting transfers between devices  70.3 us (11%)
  waiting for transfers between devices  26.1 us (4%)
  local copies, waits for them, and re-layouts  10 us (2%)
  other arithmetic  8.79 us (1%)
    psum x1, blocking collectives, body(): lax.psum((local_one, local_bias, local_two), ('gx', 'gy'))  409 us
    dot_general x108, matrix products, conv_valid(): jnp.einsum('oi,ixyz->oxyz', weight[:, :, off_x, off_y, off_z], window, pr...  67 us
    ppermute x8, starting transfers between devices, with_halo(): lax.ppermute(tail, axis, [(i, (i + 1) % count) for i in range(ends)])  33.5 us
    dot_general x54, matrix products, kernel_grad(): jnp.einsum('oxyz,ixyz->oi', cot_field, window, preferred_element_type=jnp...  32.3 us
    all_to_all x4, starting transfers between devices, full_padded(): lax.all_to_all(jnp.stack([values] * lax.axis_size('af')), 'af', 0, 0)  26.1 us
    all_to_all x4, waiting for transfers between devices, full_padded(): lax.all_to_all(jnp.stack([values] * lax.axis_size('af')), 'af', 0, 0)  22.3 us
    all_gather x1, blocking collectives, body(): lax.all_gather(weight_one, 'af', axis=0, tiled=True)  20.5 us
  transfers between devices with their start and end apart: 20, of which 4 were waited for; matrix products, arithmetic and copies ran while one was open for 8% of the time, Pallas kernels for 0%

profile of v1, /device:TPU:0, one launch (start us, length us, event | category | flops | bytes accessed | tf_op | source)
XLA Modules:
  0.0 658.8 jit_solution(257554315714373793)
XLA Ops:
  2.6 4.2 all-to-all-start.2
  6.8 14.4 %all-to-all-done.2 = bf16[4,8,4,16,128]{4,1,3,2,0:T(8,128)(2,1)S(1)} async-done(((bf16[4,8,4,16,128]{4,1,3,2,0:T(8,128)(2,1)}), bf16[4,8,4,16,128]{4,1,3,2,0:T(8,128)(2,1)S(1)}, u32[]{:S(2)}, u32[]{:S(2)}) %all-to-all-start.2) | async-done | bytes 524320 | tf_op jit(solution)/shard_map/all_to_all | solution.py:75
  22.1 3.5 all-to-all-start
  25.6 20.5 %all_gather.6 = bf16[32,32,3,3,3]{1,0,4,3,2:T(8,128)(2,1)S(1)} all-gather(bf16[8,32,3,3,3]{1,0,4,3,2:T(8,128)(2,1)S(1)} %copy-done.50), channel_id=1, replica_groups=mesh['gx'=8,'gy'=8,'af'=4] {'af'}, dimensions={0}, use_global_device_ids=true | all-gather | bytes 69120 | tf_op jit(solution)/shard_map/all_gather | solution.py:95
  46.4 12.8 %all_gather.7 = bf16[32,32,3,3,3]{1,0,4,3,2:T(8,128)(2,1)S(1)} all-gather(bf16[8,32,3,3,3]{1,0,4,3,2:T(8,128)(2,1)S(1)} %copy-done.48), channel_id=1, replica_groups=mesh['gx'=8,'gy'=8,'af'=4] {'af'}, dimensions={0}, use_global_device_ids=true | all-gather | bytes 69120 | tf_op jit(solution)/shard_map/all_gather | solution.py:96
  62.9 4.8 collective-permute-start
  70.2 3.4 collective-permute-start.10
  75.0 4.5 collective-permute-start.2
  83.3 2.2 collective-permute-done.3
  87.0 1.7 fusion.10
  98.8 1.7 select_maximum_fusion.4
  116.2 1.8 multiply_convert_fusion
  118.9 13.6 %all-to-all-start.1 = ((bf16[4,8,4,16,128]{4,1,3,2,0:T(8,128)(2,1)}), bf16[4,8,4,16,128]{4,1,3,2,0:T(8,128)(2,1)}, u32[]{:S(2)}, u32[]{:S(2)}) async-start(bf16[4,8,4,16,128]{4,1,3,2,0:T(8,128)(2,1)} %stack.197), calls=%async_computation.1 | async-start | bytes 1048576 | tf_op jit(solution)/shard_map/all_to_all | solution.py:75
  132.7 2.3 fusion.81
  135.5 1.8 convert_reduce_fusion
  159.2 4.8 all-to-all-start.3
  167.9 1.7 collective-permute-start.4
  170.9 7.9 %all-to-all-done.3 = bf16[4,8,4,16,128]{4,1,3,2,0:T(8,128)(2,1)S(1)} async-done(((bf16[4,8,4,16,128]{4,1,3,2,0:T(8,128)(2,1)}), bf16[4,8,4,16,128]{4,1,3,2,0:T(8,128)(2,1)S(1)}, u32[]{:S(2)}, u32[]{:S(2)}) %all-to-all-start.3) | async-done | bytes 524320 | tf_op jit(solution)/shard_map/all_to_all | solution.py:75
  183.7 6.3 collective-permute-start.6
  191.3 10.1 %collective-permute-start.14 = (bf16[32,6,1,128]{3,0,2,1:T(8,128)(2,1)S(1)}, bf16[32,6,1,128]{3,0,2,1:T(8,128)(2,1)S(1)}, u32[]{:S(2)}, u32[]{:S(2)}) collective-permute-start(bf16[32,6,1,128]{3,0,2,1:T(8,128)(2,1)S(1)} %get-tuple-element.20), channel_id=1, source_target_pairs={{0,4},{4,8},{8,12},{12,16},{16,20},{20,24},{24,28},{1,5},{5,9},{9,... | collective-permute-start | bytes 147464 | tf_op jit(solution)/shard_map/ppermute | solution.py:16
  205.5 1.7 select_maximum_fusion.8
  217.3 1.8 select_maximum_fusion
  244.8 409.1 %all-reduce.4 = (f32[8,32,3,3,3]{1,0,4,3,2:T(8,128)S(1)}, f32[8]{0:T(128)S(1)}, f32[8,32,3,3,3]{1,0,4,3,2:T(8,128)S(1)}) all-reduce(f32[8,32,3,3,3]{1,0,4,3,2:T(8,128)} %bitcast.436, f32[8]{0:T(128)S(1)} %get-tuple-element.44, f32[8,32,3,3,3]{1,0,4,3,2:T(8,128)} %bitcast.1445), channel_id=1, replica_groups=mesh['gx'=8,'gy'=8,'af'=4] {'gx','gy'}, use_global_device_ids=true, to_apply=%region_0.1 | all-reduce | flops 13832 | bytes 110656 | tf_op jit(solution)/shard_map/psum | solution.py:110
  654.5 2.1 fusion.105
  (325 shorter events, 118.1 us)
Async XLA Ops:
  2.6 18.6 %all-to-all-start.2 = ((bf16[4,8,4,16,128]{4,1,3,2,0:T(8,128)(2,1)}), bf16[4,8,4,16,128]{4,1,3,2,0:T(8,128)(2,1)S(1)}, u32[]{:S(2)}, u32[]{:S(2)}) async-start(bf16[4,8,4,16,128]{4,1,3,2,0:T(8,128)(2,1)} %stack.198), calls=%async_computation.2 | async-start | bytes 1048576 | tf_op jit(solution)/shard_map/all_to_all | solution.py:75
  6.7 39.6 %copy-start.48 = (bf16[8,32,3,3,3]{1,0,4,3,2:T(8,128)(2,1)S(1)}, bf16[8,32,3,3,3]{1,0,4,3,2:T(8,128)(2,1)}, u32[]{:S(2)}) copy-start(bf16[8,32,3,3,3]{1,0,4,3,2:T(8,128)(2,1)} %param.8) | copy-start | bytes 41476
  22.1 40.6 %all-to-all-start = ((bf16[4,8,4,16,128]{4,1,3,2,0:T(8,128)(2,1)}), bf16[4,8,4,16,128]{4,1,3,2,0:T(8,128)(2,1)S(1)}, u32[]{:S(2)}, u32[]{:S(2)}) async-start(bf16[4,8,4,16,128]{4,1,3,2,0:T(8,128)(2,1)} %stack.196), calls=%async_computation | async-start | bytes 1048576 | tf_op jit(solution)/shard_map/all_to_all | solution.py:75
  60.0 37.9 %copy-start.46 = (bf16[8,32,3,3,3]{1,0,4,3,2:T(8,128)(2,1)}, bf16[8,32,3,3,3]{1,0,4,3,2:T(8,128)(2,1)S(1)}, u32[]{:S(2)}) copy-start(bf16[8,32,3,3,3]{1,0,4,3,2:T(8,128)(2,1)S(1)} %dynamic-slice_bitcast_fusion) | copy-start | bytes 41476
  60.1 10.0 %collective-permute-start.8 = (bf16[32,1,16,128]{3,0,2,1:T(8,128)(2,1)S(1)}, bf16[32,1,16,128]{3,0,2,1:T(8,128)(2,1)S(1)}, u32[]{:S(2)}, u32[]{:S(2)}) collective-permute-start(bf16[32,1,16,128]{3,0,2,1:T(8,128)(2,1)S(1)} %get-tuple-element.36), channel_id=1, source_target_pairs={{0,32},{32,64},{64,96},{96,128},{128,160},{160,192},{192,224},{1,3... | collective-permute-start | bytes 393224 | tf_op jit(solution)/shard_map/ppermute | solution.py:16
  61.4 8.7 %collective-permute-start.9 = (bf16[32,1,16,128]{3,0,2,1:T(8,128)(2,1)S(1)}, bf16[32,1,16,128]{3,0,2,1:T(8,128)(2,1)S(1)}, u32[]{:S(2)}, u32[]{:S(2)}) collective-permute-start(bf16[32,1,16,128]{3,0,2,1:T(8,128)(2,1)S(1)} %get-tuple-element.37), channel_id=1, source_target_pairs={{32,0},{64,32},{96,64},{128,96},{160,128},{192,160},{224,192},{33,... | collective-permute-start | bytes 393224 | tf_op jit(solution)/shard_map/ppermute | solution.py:18
  62.9 12.0 %collective-permute-start = (bf16[32,1,16,128]{3,0,2,1:T(8,128)(2,1)S(1)}, bf16[32,1,16,128]{3,0,2,1:T(8,128)(2,1)S(1)}, u32[]{:S(2)}, u32[]{:S(2)}) collective-permute-start(bf16[32,1,16,128]{3,0,2,1:T(8,128)(2,1)S(1)} %get-tuple-element.40), channel_id=1, source_target_pairs={{0,32},{32,64},{64,96},{96,128},{128,160},{160,192},{192,224},{1,3... | collective-permute-start | bytes 393224 | tf_op jit(solution)/shard_map/ppermute | solution.py:16
  67.8 7.2 %collective-permute-start.1 = (bf16[32,1,16,128]{3,0,2,1:T(8,128)(2,1)S(1)}, bf16[32,1,16,128]{3,0,2,1:T(8,128)(2,1)S(1)}, u32[]{:S(2)}, u32[]{:S(2)}) collective-permute-start(bf16[32,1,16,128]{3,0,2,1:T(8,128)(2,1)S(1)} %get-tuple-element.41), channel_id=1, source_target_pairs={{32,0},{64,32},{96,64},{128,96},{160,128},{192,160},{224,192},{33,... | collective-permute-start | bytes 393224 | tf_op jit(solution)/shard_map/ppermute | solution.py:18
  70.2 23.0 %collective-permute-start.10 = (bf16[32,6,1,128]{3,0,2,1:T(8,128)(2,1)S(1)}, bf16[32,6,1,128]{3,0,2,1:T(8,128)(2,1)S(1)}, u32[]{:S(2)}, u32[]{:S(2)}) collective-permute-start(bf16[32,6,1,128]{3,0,2,1:T(8,128)(2,1)S(1)} %get-tuple-element.24), channel_id=1, source_target_pairs={{0,4},{4,8},{8,12},{12,16},{16,20},{20,24},{24,28},{1,5},{5,9},{9,... | collective-permute-start | bytes 147464 | tf_op jit(solution)/shard_map/ppermute | solution.py:16
  73.6 19.6 %collective-permute-start.11 = (bf16[32,6,1,128]{3,0,2,1:T(8,128)(2,1)S(1)}, bf16[32,6,1,128]{3,0,2,1:T(8,128)(2,1)S(1)}, u32[]{:S(2)}, u32[]{:S(2)}) collective-permute-start(bf16[32,6,1,128]{3,0,2,1:T(8,128)(2,1)S(1)} %get-tuple-element.25), channel_id=1, source_target_pairs={{4,0},{8,4},{12,8},{16,12},{20,16},{24,20},{28,24},{5,1},{9,5},{13... | collective-permute-start | bytes 147464 | tf_op jit(solution)/shard_map/ppermute | solution.py:18
  75.0 8.4 %collective-permute-start.2 = (bf16[32,6,1,128]{3,0,2,1:T(8,128)(2,1)S(1)}, bf16[32,6,1,128]{3,0,2,1:T(8,128)(2,1)S(1)}, u32[]{:S(2)}, u32[]{:S(2)}) collective-permute-start(bf16[32,6,1,128]{3,0,2,1:T(8,128)(2,1)S(1)} %get-tuple-element.32), channel_id=1, source_target_pairs={{0,4},{4,8},{8,12},{12,16},{16,20},{20,24},{24,28},{1,5},{5,9},{9,... | collective-permute-start | bytes 147464 | tf_op jit(solution)/shard_map/ppermute | solution.py:16
  79.5 6.0 collective-permute-start.3
  118.9 39.4 %all-to-all-start.1 = ((bf16[4,8,4,16,128]{4,1,3,2,0:T(8,128)(2,1)}), bf16[4,8,4,16,128]{4,1,3,2,0:T(8,128)(2,1)}, u32[]{:S(2)}, u32[]{:S(2)}) async-start(bf16[4,8,4,16,128]{4,1,3,2,0:T(8,128)(2,1)} %stack.197), calls=%async_computation.1 | async-start | bytes 1048576 | tf_op jit(solution)/shard_map/all_to_all | solution.py:75
  159.2 19.6 %all-to-all-start.3 = ((bf16[4,8,4,16,128]{4,1,3,2,0:T(8,128)(2,1)}), bf16[4,8,4,16,128]{4,1,3,2,0:T(8,128)(2,1)S(1)}, u32[]{:S(2)}, u32[]{:S(2)}) async-start(bf16[4,8,4,16,128]{4,1,3,2,0:T(8,128)(2,1)} %stack.199), calls=%async_computation.3 | async-start | bytes 1048576 | tf_op jit(solution)/shard_map/all_to_all | solution.py:75
  167.9 15.8 %collective-permute-start.4 = (bf16[32,1,16,128]{3,0,2,1:T(8,128)(2,1)S(1)}, bf16[32,1,16,128]{3,0,2,1:T(8,128)(2,1)S(1)}, u32[]{:S(2)}, u32[]{:S(2)}) collective-permute-start(bf16[32,1,16,128]{3,0,2,1:T(8,128)(2,1)S(1)} %get-tuple-element.38), channel_id=1, source_target_pairs={{0,32},{32,64},{64,96},{96,128},{128,160},{160,192},{192,224},{1,3... | collective-permute-start | bytes 393224 | tf_op jit(solution)/shard_map/ppermute | solution.py:16
  169.6 14.1 %collective-permute-start.5 = (bf16[32,1,16,128]{3,0,2,1:T(8,128)(2,1)S(1)}, bf16[32,1,16,128]{3,0,2,1:T(8,128)(2,1)S(1)}, u32[]{:S(2)}, u32[]{:S(2)}) collective-permute-start(bf16[32,1,16,128]{3,0,2,1:T(8,128)(2,1)S(1)} %get-tuple-element.39), channel_id=1, source_target_pairs={{32,0},{64,32},{96,64},{128,96},{160,128},{192,160},{224,192},{33,... | collective-permute-start | bytes 393224 | tf_op jit(solution)/shard_map/ppermute | solution.py:18
  178.9 12.3 %collective-permute-start.12 = (bf16[32,1,16,128]{3,0,2,1:T(8,128)(2,1)S(1)}, bf16[32,1,16,128]{3,0,2,1:T(8,128)(2,1)S(1)}, u32[]{:S(2)}, u32[]{:S(2)}) collective-permute-start(bf16[32,1,16,128]{3,0,2,1:T(8,128)(2,1)S(1)} %get-tuple-element.34), channel_id=1, source_target_pairs={{0,32},{32,64},{64,96},{96,128},{128,160},{160,192},{192,224},{1,3... | collective-permute-start | bytes 393224 | tf_op jit(solution)/shard_map/ppermute | solution.py:16
  180.2 11.0 %collective-permute-start.13 = (bf16[32,1,16,128]{3,0,2,1:T(8,128)(2,1)S(1)}, bf16[32,1,16,128]{3,0,2,1:T(8,128)(2,1)S(1)}, u32[]{:S(2)}, u32[]{:S(2)}) collective-permute-start(bf16[32,1,16,128]{3,0,2,1:T(8,128)(2,1)S(1)} %get-tuple-element.35), channel_id=1, source_target_pairs={{32,0},{64,32},{96,64},{128,96},{160,128},{192,160},{224,192},{33,... | collective-permute-start | bytes 393224 | tf_op jit(solution)/shard_map/ppermute | solution.py:18
  183.7 20.5 %collective-permute-start.6 = (bf16[32,6,1,128]{3,0,2,1:T(8,128)(2,1)S(1)}, bf16[32,6,1,128]{3,0,2,1:T(8,128)(2,1)S(1)}, u32[]{:S(2)}, u32[]{:S(2)}) collective-permute-start(bf16[32,6,1,128]{3,0,2,1:T(8,128)(2,1)S(1)} %get-tuple-element.28), channel_id=1, source_target_pairs={{0,4},{4,8},{8,12},{12,16},{16,20},{20,24},{24,28},{1,5},{5,9},{9,... | collective-permute-start | bytes 147464 | tf_op jit(solution)/shard_map/ppermute | solution.py:16
  190.0 14.2 %collective-permute-start.7 = (bf16[32,6,1,128]{3,0,2,1:T(8,128)(2,1)S(1)}, bf16[32,6,1,128]{3,0,2,1:T(8,128)(2,1)S(1)}, u32[]{:S(2)}, u32[]{:S(2)}) collective-permute-start(bf16[32,6,1,128]{3,0,2,1:T(8,128)(2,1)S(1)} %get-tuple-element.29), channel_id=1, source_target_pairs={{4,0},{8,4},{12,8},{16,12},{20,16},{24,20},{28,24},{5,1},{9,5},{13... | collective-permute-start | bytes 147464 | tf_op jit(solution)/shard_map/ppermute | solution.py:18
  191.3 20.3 %collective-permute-start.14 = (bf16[32,6,1,128]{3,0,2,1:T(8,128)(2,1)S(1)}, bf16[32,6,1,128]{3,0,2,1:T(8,128)(2,1)S(1)}, u32[]{:S(2)}, u32[]{:S(2)}) collective-permute-start(bf16[32,6,1,128]{3,0,2,1:T(8,128)(2,1)S(1)} %get-tuple-element.20), channel_id=1, source_target_pairs={{0,4},{4,8},{8,12},{12,16},{16,20},{20,24},{24,28},{1,5},{5,9},{9,... | collective-permute-start | bytes 147464 | tf_op jit(solution)/shard_map/ppermute | solution.py:16
  201.4 11.7 %collective-permute-start.15 = (bf16[32,6,1,128]{3,0,2,1:T(8,128)(2,1)S(1)}, bf16[32,6,1,128]{3,0,2,1:T(8,128)(2,1)S(1)}, u32[]{:S(2)}, u32[]{:S(2)}) collective-permute-start(bf16[32,6,1,128]{3,0,2,1:T(8,128)(2,1)S(1)} %get-tuple-element.21), channel_id=1, source_target_pairs={{4,0},{8,4},{12,8},{16,12},{20,16},{24,20},{28,24},{5,1},{9,5},{13... | collective-permute-start | bytes 147464 | tf_op jit(solution)/shard_map/ppermute | solution.py:18
  243.7 410.7 %copy-start.43 = (f32[8,4,16,128]{3,0,2,1:T(8,128)S(1)}, f32[8,4,16,128]{3,0,2,1:T(8,128)}, u32[]{:S(2)}) copy-start(f32[8,4,16,128]{3,0,2,1:T(8,128)} %fusion.383) | copy-start | bytes 786436
  243.7 410.7 %copy-start.44 = (f32[8,4,16,128]{3,0,2,1:T(8,128)S(1)}, f32[8,4,16,128]{3,0,2,1:T(8,128)}, u32[]{:S(2)}) copy-start(f32[8,4,16,128]{3,0,2,1:T(8,128)} %fusion.234) | copy-start | bytes 786436
  (50 other events, 327.6 us)
